TPU v7x, 32 devices: a whole 2x2x4 slice. The times are simulated.
32 devices in a mesh: req: 8 (over z, x), tp: 4 (over y, core).
Axes of the slice: x: 2, y: 2, z: 4, core: 2. Of those that a mesh axis runs over, the one named last changes fastest.
Arguments:
- queries: bfloat16 [256, 7168], P('req', 'tp')
- new_keys: bfloat16 [256, 1024], P('req', 'tp'), may hold values from -6 to 6
- new_values: bfloat16 [256, 1024], P('req', 'tp'), may hold values from -6 to 6
- cache_keys: bfloat16 [143360, 1024], P('req', 'tp'), may hold values from -6 to 6
- cache_values: bfloat16 [143360, 1024], P('req', 'tp'), may hold values from -6 to 6
- tok_req: int32 [256], P('req'), may hold values from 0 to 16, as said below
- cache_req: int32 [143360], P('req'), may hold values from -1 to 16, as said below
- out_weight: bfloat16 [7168, 7168], P('tp', 'req'), may hold values from -0.0625 to 0.0625
- residual: bfloat16 [256, 7168], P('tp', 'req')
- norm_gain: float32 [7168], replicated, may hold values from 0.1 to 1.9
- gate_weight: bfloat16 [7168, 20480], P(None, ('req', 'tp')), may hold values from -0.0625 to 0.0625
- up_weight: bfloat16 [7168, 20480], P(None, ('req', 'tp')), may hold values from -0.0625 to 0.0625
- down_weight: bfloat16 [20480, 7168], P(('req', 'tp')), may hold values from -0.078125 to 0.078125
Outputs:
- layer_out: bfloat16 [256, 7168], P('tp', 'req')
Inputs may be any that keep to these rules, and one draw needn't show every extreme that they name: `tok_req`: within a group, request 0 is the prefill request, whose tokens stand first and in order; decode requests 1, 2, ... follow with one token each. `cache_req`: -1 marks an empty slot; within a group the owned slots stand first, each request's slots together, requests in increasing order; every request of a group that has tokens owns at least one slot.
All inputs are finite; a program needn't handle non-finite values.
Results may differ from a plain program's by a relative error of at most 0.014.
Values may be sent and summed in bfloat16 or wider, within the bound.
A program may use at most 128 MiB of HBM per device.

v0:
```python
import math

import jax
import jax.numpy as jnp
from jax import lax
from jax.sharding import PartitionSpec as P

HD = 128


epsilon = 1e-05
masked_value = -1e30
key_block = 512


def attend(queries, new_keys, new_values, cache_keys, cache_values, tok_req, cache_req):
    tokens_here = queries.shape[0]
    head_dim = HD
    kv_here = new_keys.shape[1] // head_dim
    group_size = queries.shape[1] // (kv_here * head_dim)
    score_scale = 1.0 / math.sqrt(head_dim)
    row_count = tokens_here * group_size
    grouped = queries.reshape(tokens_here, kv_here, group_size, head_dim)
    row_req = jnp.repeat(tok_req, group_size)
    row_tok = jnp.repeat(jnp.arange(tokens_here, dtype=jnp.int32), group_size)
    pool_size = cache_keys.shape[0]
    block_width = min(key_block, pool_size)
    live_slots = jnp.sum((cache_req >= 0).astype(jnp.int32))
    live_blocks = (live_slots + block_width - 1) // block_width

    def update(carried, block_keys, block_values, visible):
        renewed = []
        for kv_head in range(kv_here):
            running_max, denominator, weighted = carried[kv_head]
            query_rows = grouped[:, kv_head].reshape(row_count, head_dim)
            head_keys = block_keys[:, kv_head * head_dim : (kv_head + 1) * head_dim]
            head_values = block_values[:, kv_head * head_dim : (kv_head + 1) * head_dim]
            scores = (
                jnp.einsum("qd,kd->qk", query_rows, head_keys, preferred_element_type=jnp.float32)
                * score_scale
            )
            masked = jnp.where(visible, scores, masked_value)
            new_max = jnp.maximum(running_max, jnp.max(masked, axis=1))
            weights = jnp.where(visible, jnp.exp(masked - new_max[:, None]), 0.0).astype(
                jnp.bfloat16
            )
            factor = jnp.exp(running_max - new_max)
            denominator = denominator * factor + jnp.sum(weights.astype(jnp.float32), axis=1)
            weighted = weighted * factor[:, None] + jnp.dot(
                weights, head_values, preferred_element_type=jnp.float32
            )
            renewed.append((new_max, denominator, weighted))
        return tuple(renewed)

    initial = tuple(
        (
            (
                jnp.full((row_count,), masked_value, jnp.float32),
                jnp.zeros((row_count,), jnp.float32),
                jnp.zeros((row_count, head_dim), jnp.float32),
            )
            for unused in range(kv_here)
        )
    )

    def consume(block_index, carried):
        first_slot = block_index * block_width
        block_keys = lax.dynamic_slice_in_dim(cache_keys, first_slot, block_width, 0)
        block_values = lax.dynamic_slice_in_dim(cache_values, first_slot, block_width, 0)
        owners = lax.dynamic_slice_in_dim(cache_req, first_slot, block_width, 0)
        visible = owners[None, :] == row_req[:, None]
        return update(carried, block_keys, block_values, visible)

    carried = lax.fori_loop(0, live_blocks, consume, initial)
    causal = (tok_req[None, :] == row_req[:, None]) & (
        jnp.arange(tokens_here, dtype=jnp.int32)[None, :] <= row_tok[:, None]
    )
    carried = update(carried, new_keys, new_values, causal)
    per_head = [
        (weighted / denominator[:, None]).reshape(tokens_here, group_size, head_dim)
        for running_max, denominator, weighted in carried
    ]
    return (
        jnp.stack(per_head, axis=1)
        .reshape(tokens_here, kv_here * group_size * head_dim)
        .astype(jnp.bfloat16)
    )


def per_device(
    queries,
    new_keys,
    new_values,
    cache_keys,
    cache_values,
    tok_req,
    cache_req,
    out_weight,
    residual,
    norm_gain,
    gate_weight,
    up_weight,
    down_weight,
):
    attended = attend(queries, new_keys, new_values, cache_keys, cache_values, tok_req, cache_req)
    partial_out = jnp.dot(
        lax.all_gather(attended, "req", axis=0, tiled=True),
        out_weight,
        preferred_element_type=jnp.float32,
    )
    mixed = lax.psum_scatter(
        partial_out.astype(jnp.bfloat16), "tp", scatter_dimension=0, tiled=True
    ).astype(jnp.float32)
    stream = (residual.astype(jnp.float32) + mixed).astype(jnp.bfloat16)
    group_count = lax.axis_size("req")
    columns = stream.shape[1]
    model_width = columns * group_count
    hidden_here = gate_weight.shape[1]
    total_tokens = stream.shape[0] * lax.axis_size("tp")
    gate_blocks = gate_weight.reshape(group_count, columns, hidden_here)
    up_blocks = up_weight.reshape(group_count, columns, hidden_here)
    own_gain = lax.dynamic_slice_in_dim(norm_gain, lax.axis_index("req") * columns, columns, 0)
    wide = stream.astype(jnp.float32)
    squares = lax.psum(jnp.sum(wide * wide, axis=1), "req")
    normed = (
        wide * lax.rsqrt(squares / model_width + epsilon)[:, None] * own_gain[None, :]
    ).astype(jnp.bfloat16)
    zeros = jnp.zeros((total_tokens, hidden_here), jnp.float32)
    shard_rows = lax.all_gather(normed, ("req", "tp"), axis=0, tiled=True)
    piece_rows = shard_rows.shape[0]
    sub_rows = math.gcd(piece_rows, total_tokens)
    sub_count = piece_rows // sub_rows
    offsets = jnp.arange(sub_count, dtype=jnp.int32) * sub_rows
    column_ids = offsets // total_tokens
    token_ids = offsets % total_tokens // sub_rows
    pieces = shard_rows.reshape(sub_count, sub_rows, columns)
    gate_part = jnp.einsum(
        "nsk,nkf->nsf", pieces, gate_blocks[column_ids], preferred_element_type=jnp.float32
    )
    up_part = jnp.einsum(
        "nsk,nkf->nsf", pieces, up_blocks[column_ids], preferred_element_type=jnp.float32
    )
    gate_sum = (
        zeros.reshape(total_tokens // sub_rows, sub_rows, hidden_here).at[token_ids].add(gate_part)
    )
    up_sum = (
        zeros.reshape(total_tokens // sub_rows, sub_rows, hidden_here).at[token_ids].add(up_part)
    )
    gate = gate_sum.reshape(total_tokens, hidden_here)
    up = up_sum.reshape(total_tokens, hidden_here)
    hidden = (jax.nn.silu(gate) * up).astype(jnp.bfloat16)
    down_blocks = down_weight.reshape(hidden_here, group_count, columns)
    sub_rows = math.gcd(
        total_tokens // lax.axis_size("tp") * lax.axis_size(("req", "tp")), total_tokens
    )
    sub_count = total_tokens // lax.axis_size("tp") * lax.axis_size(("req", "tp")) // sub_rows
    offsets = jnp.arange(sub_count, dtype=jnp.int32) * sub_rows
    column_ids = offsets // total_tokens
    token_ids = offsets % total_tokens // sub_rows
    hidden_rows = hidden.reshape(total_tokens // sub_rows, sub_rows, hidden_here)[token_ids]
    block_weights = jnp.take(down_blocks, column_ids, axis=1)
    product = jnp.einsum(
        "nsf,fnd->nsd", hidden_rows, block_weights, preferred_element_type=jnp.float32
    )
    summed = lax.psum_scatter(
        product.reshape(
            total_tokens // lax.axis_size("tp") * lax.axis_size(("req", "tp")), columns
        ),
        ("req", "tp"),
        scatter_dimension=0,
        tiled=True,
    )
    return (stream.astype(jnp.float32) + summed).astype(jnp.bfloat16)


def solution(mesh):
    in_specs = (
        P("req", "tp"),
        P("req", "tp"),
        P("req", "tp"),
        P("req", "tp"),
        P("req", "tp"),
        P("req"),
        P("req"),
        P("tp", "req"),
        P("tp", "req"),
        P(),
        P(None, ("req", "tp")),
        P(None, ("req", "tp")),
        P(("req", "tp"), None),
    )
    out_specs = P("tp", "req")
    return jax.shard_map(
        per_device, mesh=mesh, in_specs=in_specs, out_specs=out_specs, check_vma=False
    )
```

profile of v0, /device:TPU:0, one launch (start us, length us, event | category | flops | bytes accessed | tf_op | source)
XLA Modules:
  0.0 610.0 jit_solution(700358703328336462)
XLA Ops:
  11.9 89.0 %while.21 = (s32[]{:T(128)}, f32[224]{0:T(256)S(1)}, f32[224]{0:T(256)S(1)}, f32[224,128]{1,0:T(8,128)}, f32[224]{0:T(256)S(1)}, /*index=5*/f32[224]{0:T(256)S(1...) while((s32[]{:T(128)}, f32[224]{0:T(256)S(1)}, ...), condition=%wide.region_6.7_spmd.clone, body=%wide.region_1.6_spmd.clone.sunk | while | flops 119735168 | bytes 4351867 | solution.py:74
  13.6 1.9 fusion.84
  23.5 1.9 fusion.84
  33.4 1.9 fusion.84
  43.3 1.9 fusion.84
  53.2 1.9 fusion.84
  63.0 1.9 fusion.84
  82.8 1.9 fusion.84
  110.1 198.3 %all_gather.6 = bf16[256,1792]{1,0:T(8,128)(2,1)S(1)} all-gather(bf16[32,1792]{1,0:T(8,128)(2,1)} %convert_element_type.63), channel_id=1, replica_groups=mesh['req'=8,'tp'=4] {'req'}, dimensions={0}, use_global_device_ids=true | all-gather | bytes 1032192 | tf_op jit(solution)/shard_map/all_gather | solution.py:107
  308.4 1.9 convolution_convert_fusion
  311.2 21.0 %reduce-scatter.3.cloned.1.call-done = bf16[64,896]{1,0:T(8,128)(2,1)} async-done(((bf16[256,896]{1,0:T(8,128)(2,1)}), bf16[64,896]{1,0:T(8,128)(2,1)}) %reduce-scatter.3.cloned.1.call-update) | async-done | bytes 114704 | tf_op jit(solution)/shard_map/reduce_scatter | solution.py:111
  333.3 21.4 %psum.7 = f32[64]{0:T(128)S(1)} all-reduce(f32[64]{0:T(128)S(1)} %fusion.31), channel_id=1, replica_groups=mesh['req'=8,'tp'=4] {'req'}, use_global_device_ids=true, to_apply=%region_13.14 | all-reduce | flops 64 | bytes 512 | tf_op jit(solution)/shard_map/psum | solution.py:124
  356.5 8.9 %gather_fusion = bf16[8,896,640]{2,1,0:T(8,128)(2,1)} fusion(bf16[8,896,640]{2,1,0:T(8,128)(2,1)} %bitcast.70, s32[1024]{0:T(1024)S(1)} %pad_clamp_fusion), kind=kCustom, calls=%fused_computation | custom fusion | bytes 18350112 | tf_op jit(solution)/shard_map/gather | solution.py:138
  365.5 8.9 %gather_fusion.1 = bf16[8,896,640]{2,1,0:T(8,128)(2,1)} fusion(bf16[8,896,640]{2,1,0:T(8,128)(2,1)} %bitcast.71, s32[1024]{0:T(1024)S(1)} %pad_clamp_fusion), kind=kCustom, calls=%fused_computation.1 | custom fusion | bytes 18350112 | tf_op jit(solution)/shard_map/gather | solution.py:141
  374.4 12.8 %copy.18 = bf16[640,7168]{0,1:T(8,128)(2,1)} copy(bf16[640,7168]{1,0:T(8,128)(2,1)} %param.27) | data formatting | bytes 18350080 | tf_op args[12]
  387.1 12.9 %copy.19 = bf16[640,8,896]{2,0,1:T(8,128)(2,1)} copy(bf16[640,8,896]{0,2,1:T(8,128)(2,1)} %bitcast.67) | data formatting | bytes 18350080 | tf_op jit(solution)/shard_map/reshape | solution.py:152
  400.0 8.9 %gather_fusion.2 = bf16[8,640,896]{2,1,0:T(8,128)(2,1)} fusion(bf16[640,8,896]{2,0,1:T(8,128)(2,1)} %copy.19, s32[1024]{0:T(1024)S(1)} %pad_clamp_fusion), kind=kCustom, calls=%fused_computation.2 | custom fusion | bytes 18350112 | tf_op jit(solution)/shard_map/jit(_take)/gather | solution.py:161
  409.0 4.3 all-gather.2.cloned.1.call-done
  413.2 10.5 %fusion.53 = f32[8,256,640]{2,1,0:T(8,128)} fusion(bf16[8,256,896]{2,1,0:T(8,128)(2,1)} %bitcast.68, bf16[8,896,640]{2,1,0:T(8,128)(2,1)} %gather_fusion), kind=kOutput, calls=%fused_computation.109 | convolution fusion | flops 2348810240 | bytes 18087936 | tf_op jit(solution)/shard_map/nsk,nkf->nsf/dot_general | solution.py:137
  423.7 8.9 %fusion.54 = f32[8,256,640]{2,1,0:T(8,128)} fusion(bf16[8,256,896]{2,1,0:T(8,128)(2,1)S(1)} %bitcast.69, bf16[8,896,640]{2,1,0:T(8,128)(2,1)} %gather_fusion.1), kind=kOutput, calls=%fused_computation.110 | convolution fusion | flops 2348810240 | bytes 18087936 | tf_op jit(solution)/shard_map/nsk,nkf->nsf/dot_general | solution.py:140
  432.7 6.3 %scatter_fusion = f32[256,640,1]{1,0,2:T(8,128)S(1)} fusion(f32[256,640,1]{1,0,2:T(8,128)S(1)} %broadcast.283.clone.1, s32[8]{0:T(128)S(1)} %fusion.40, f32[8,256,640]{2,1,0:T(8,128)} %fusion.53), kind=kCustom, calls=%fused_computation.3 | custom fusion | flops 1310720 | bytes 15728672 | tf_op jit(solution)/shard_map/scatter-add | solution.py:144
  439.1 6.3 %scatter_fusion.1 = f32[256,640,1]{1,0,2:T(8,128)S(1)} fusion(f32[256,640,1]{1,0,2:T(8,128)S(1)} %broadcast.283.clone, s32[8]{0:T(128)S(1)} %fusion.40, f32[8,256,640]{2,1,0:T(8,128)} %fusion.54), kind=kCustom, calls=%fused_computation.4 | custom fusion | flops 1310720 | bytes 15728672 | tf_op jit(solution)/shard_map/scatter-add | solution.py:147
  445.7 9.7 %fusion.14 = f32[8,256,896]{2,1,0:T(8,128)} fusion(bf16[8,640,896]{2,1,0:T(8,128)(2,1)} %gather_fusion.2, pred[8]{0:T(512)(128)(4,1)S(1)} %compare_and_fusion, bf16[256,640]{1,0:T(8,128)(2,1)S(1)} %fusion.30), kind=kOutput, calls=%fused_computation.30 | convolution fusion | flops 2353397760 | bytes 16842760 | tf_op jit(solution)/shard_map/nsf,fnd->nsd/dot_general | solution.py:162
  455.3 146.5 %reduce-scatter.5.cloned.1.call-done = f32[64,896]{1,0:T(8,128)} async-done(((f32[2048,896]{1,0:T(8,128)}), f32[64,896]{1,0:T(8,128)}) %reduce-scatter.5.cloned.1.call-update) | async-done | bytes 229392 | tf_op jit(solution)/shard_map/reduce_scatter | solution.py:165
  (196 shorter events, 94.8 us)
Async XLA Ops:
  6.5 301.9 %copy-start = (bf16[1792,896]{1,0:T(8,128)(2,1)S(1)}, bf16[1792,896]{1,0:T(8,128)(2,1)}, u32[]{:S(2)}) copy-start(bf16[1792,896]{1,0:T(8,128)(2,1)} %param.22) | copy-start | bytes 9633796
  6.5 325.7 %reduce-scatter.3.cloned.1.call-start = ((), (), s32[]{:S(2)}) async-start(), calls=%async_computation.2 | async-start | bytes 573440 | tf_op jit(solution)/shard_map/reduce_scatter | solution.py:111
  100.9 231.3 %copy-start.3 = (bf16[64,896]{1,0:T(8,128)(2,1)S(1)}, bf16[64,896]{1,0:T(8,128)(2,1)}, u32[]{:S(2)}) copy-start(bf16[64,896]{1,0:T(8,128)(2,1)} %param.23) | copy-start | bytes 344068
  105.4 1.4 copy-start.5
  310.3 102.9 %all-gather.2.cloned.1.call-start = ((), (), s32[]{:S(2)}) async-start(), calls=%async_computation.3 | async-start | bytes 3784704 | tf_op jit(solution)/shard_map/all_gather | solution.py:129
  356.3 245.6 %reduce-scatter.5.cloned.1.call-start = ((), (), s32[]{:S(2)}) async-start(), calls=%async_computation.4 | async-start | bytes 7569408 | tf_op jit(solution)/shard_map/reduce_scatter | solution.py:165
  413.2 10.5 %copy-start.2 = (bf16[2048,896]{1,0:T(8,128)(2,1)S(1)}, bf16[2048,896]{1,0:T(8,128)(2,1)}, u32[]{:S(2)}) copy-start(bf16[2048,896]{1,0:T(8,128)(2,1)} %all-gather.2.cloned.1.call-done) | copy-start | bytes 11010052
  445.6 156.2 %copy-start.4 = (bf16[64,896]{1,0:T(8,128)(2,1)S(1)}, bf16[64,896]{1,0:T(8,128)(2,1)}, u32[]{:S(2)}) copy-start(bf16[64,896]{1,0:T(8,128)(2,1)} %reduce-scatter.3.cloned.1.call-done) | copy-start | bytes 344068
  445.7 157.8 %copy-start.1 = (bf16[1792,896]{1,0:T(8,128)(2,1)S(1)}, bf16[1792,896]{1,0:T(8,128)(2,1)}, u32[]{:S(2)}) copy-start(bf16[1792,896]{1,0:T(8,128)(2,1)} %param.22) | copy-start | bytes 9633796
Sparse Core Ops, SparseCore 0:
  310.5 21.7 reduce-scatter.2
  356.4 56.7 all-gather.1
  455.5 146.3 reduce-scatter.4
where the time goes:
time: 611 us; the launch traced here: 610 us
  blocking collectives  220 us (36%)
  waiting for transfers between devices  172 us (28%)
  matrix products  96.1 us (16%)
  local copies, waits for them, and re-layouts  74.9 us (12%)
  other arithmetic  32.9 us (5%)
  between operations  14 us (2%)
    all_gather x1, blocking collectives, per_device(): lax.all_gather(attended, 'req', axis=0, tiled=True)  198 us
    reduce_scatter x1, waiting for transfers between devices, per_device(): lax.psum_scatter(product.reshape(total_tokens // lax.axis_size('tp') * la...  147 us
    dot_general x20, matrix products, update(): jnp.dot(weights, head_values, preferred_element_type=jnp.float32)  35.2 us
    dot_general x20, matrix products, update(): jnp.einsum('qd,kd->qk', query_rows, head_keys, preferred_element_type=jnp...  29.9 us
    psum x1, blocking collectives, per_device(): squares = lax.psum(jnp.sum(wide * wide, axis=1), 'req')  21.4 us
    reduce_scatter x1, waiting for transfers between devices, per_device(): lax.psum_scatter(partial_out.astype(jnp.bfloat16), 'tp', scatter_dimensio...  21 us
    reduce_sum x10, other arithmetic, update(): jnp.sum(weights.astype(jnp.float32), axis=1)  13.1 us
    reshape x1, local copies, waits for them, and re-layouts, per_device(): down_blocks = down_weight.reshape(hidden_here, group_count, columns)  12.9 us
  transfers between devices with their start and end apart: 3, of which 3 were waited for; matrix products, arithmetic and copies ran while one was open for 9% of the time, Pallas kernels for 0%

commit v1 on v0

v1 whole, which is shorter than its diff:
```python
import functools
import math

import jax
import jax.numpy as jnp
from jax import lax
from jax.experimental import pallas as pl
from jax.experimental.pallas import tpu as pltpu
from jax.sharding import PartitionSpec as P

HD = 128
epsilon = 1e-05
masked_value = -1e30
key_block = 512
score_factor = math.log2(math.e) / math.sqrt(HD)
BF = jnp.bfloat16
F32 = jnp.float32


def attend_kernel(
    first_ref, count_ref, bounds_ref, q_ref, nk_ref, nv_ref, ck_ref, cv_ref, out_ref,
    kbuf, vbuf, ksem, vsem, m_ref, l_ref, acc_ref,
):
    windows = q_ref.shape[0]
    kv = q_ref.shape[2] // HD
    pool = ck_ref.shape[0]
    width = kbuf.shape[1]
    slots = kbuf.shape[0]
    ahead = slots - 1

    def copies(w, b, slot):
        start = jnp.minimum(first_ref[w] + b * width, pool - width)
        start = pl.multiple_of(start, 16)
        rows = pl.ds(start, width)
        return (
            pltpu.make_async_copy(ck_ref.at[rows], kbuf.at[slot], ksem.at[slot]),
            pltpu.make_async_copy(cv_ref.at[rows], vbuf.at[slot], vsem.at[slot]),
        )

    def advance(w, b):
        last = b + 1 >= count_ref[jnp.minimum(w, windows - 1)]
        return jnp.where(last, w + 1, w), jnp.where(last, 0, b + 1)

    def fetch(w, b, slot):
        @pl.when(w < windows)
        def _():
            for c in copies(w, b, slot):
                c.start()

    w0, b0 = jnp.int32(0), jnp.int32(0)
    for i in range(ahead):
        fetch(w0, b0, i)
        w0, b0 = advance(w0, b0)

    def col(row):
        return jnp.transpose(jnp.broadcast_to(row, (8, row.shape[1])))[:, :1]

    def scores_of(keys, w, low, high):
        s = lax.dot_general(
            keys, q_ref[w], (((1,), (1,)), ((), ())), preferred_element_type=F32
        )
        pos = lax.broadcasted_iota(jnp.int32, s.shape, 0)
        return jnp.where((pos >= low) & (pos < high), s * score_factor, masked_value)

    def weigh(p, values):
        return lax.dot_general(p, values, (((0,), (0,)), ((), ())), preferred_element_type=F32)

    def window(w, carry):
        low, high = bounds_ref[w, 0:1, :], bounds_ref[w, 1:2, :]
        s = scores_of(nk_ref[...], w, bounds_ref[w, 2:3, :], bounds_ref[w, 3:4, :])
        m = jnp.max(s, axis=0, keepdims=True)
        p = jnp.exp2(s - m).astype(BF)
        m_ref[...] = m
        l_ref[...] = jnp.sum(p.astype(F32), axis=0, keepdims=True)
        acc_ref[...] = weigh(p, nv_ref[...])

        def block(b, inner):
            item, wn, bn = inner
            slot = lax.rem(item, slots)
            fetch(wn, bn, lax.rem(item + ahead, slots))
            for c in copies(w, b, slot):
                c.wait()
            nominal = first_ref[w] + b * width
            start = jnp.minimum(nominal, pool - width)
            s = scores_of(kbuf[slot], w, jnp.maximum(low, nominal) - start, high - start)
            m_old = m_ref[...]
            m_new = jnp.maximum(m_old, jnp.max(s, axis=0, keepdims=True))
            alpha = jnp.exp2(m_old - m_new)
            p = jnp.exp2(s - m_new).astype(BF)
            m_ref[...] = m_new
            l_ref[...] = l_ref[...] * alpha + jnp.sum(p.astype(F32), axis=0, keepdims=True)
            acc_ref[...] = acc_ref[...] * col(alpha) + weigh(p, vbuf[slot])
            return (item + 1, *advance(wn, bn))

        carry = lax.fori_loop(0, count_ref[w], block, carry)
        scaled = acc_ref[...] / col(l_ref[...])
        rows = scaled.shape[0] // kv
        for h in range(kv):
            part = slice(h * rows, (h + 1) * rows)
            out_ref[w, part, :] = scaled[part, h * HD : (h + 1) * HD].astype(BF)
        return carry

    lax.fori_loop(0, windows, window, (jnp.int32(0), w0, b0))


def attend(queries, new_keys, new_values, cache_keys, cache_values, tok_req, cache_req):
    tokens = queries.shape[0]
    kv = new_keys.shape[1] // HD
    group = queries.shape[1] // (kv * HD)
    padded = (group + 7) // 8 * 8
    span = max(1, min(tokens, 128 // (padded * kv)))
    windows = tokens // span
    columns = kv * span * padded
    depth = kv * HD
    pool = cache_keys.shape[0]
    width = min(key_block, pool)

    owned = cache_req[None, :] >= 0
    low = jnp.sum((owned & (cache_req[None, :] < tok_req[:, None])).astype(jnp.int32), axis=1)
    high = jnp.sum((owned & (cache_req[None, :] <= tok_req[:, None])).astype(jnp.int32), axis=1)
    new_low = jnp.sum((tok_req[None, :] < tok_req[:, None]).astype(jnp.int32), axis=1)
    new_high = jnp.arange(1, tokens + 1, dtype=jnp.int32)
    first = jnp.min(low.reshape(windows, span), axis=1) // 16 * 16
    last = jnp.max(high.reshape(windows, span), axis=1)
    count = jnp.maximum((last - first + width - 1) // width, 1)
    bounds = jnp.stack([low, high, new_low, new_high] * 2)
    bounds = bounds.reshape(8, windows, 1, span, 1).transpose(1, 0, 2, 3, 4)
    bounds = jnp.broadcast_to(bounds, (windows, 8, kv, span, padded)).reshape(windows, 8, columns)

    q = queries.reshape(windows, span, kv, group, HD)
    q = jnp.pad(q, ((0, 0), (0, 0), (0, 0), (0, padded - group), (0, 0)))
    q = q.transpose(0, 2, 1, 3, 4).reshape(windows, kv, span * padded, 1, HD)
    q = q * jnp.eye(kv, dtype=BF)[None, :, None, :, None]
    q = q.reshape(windows, columns, depth)

    vmem = pl.BlockSpec(memory_space=pltpu.VMEM)
    smem = pl.BlockSpec(memory_space=pltpu.SMEM)
    anywhere = pl.BlockSpec(memory_space=pl.ANY)
    slots = 4
    out = pl.pallas_call(
        attend_kernel,
        out_shape=jax.ShapeDtypeStruct((windows, columns, HD), BF),
        in_specs=[smem, smem, vmem, vmem, vmem, vmem, anywhere, anywhere],
        out_specs=vmem,
        scratch_shapes=[
            pltpu.VMEM((slots, width, depth), BF),
            pltpu.VMEM((slots, width, depth), BF),
            pltpu.SemaphoreType.DMA((slots,)),
            pltpu.SemaphoreType.DMA((slots,)),
            pltpu.VMEM((1, columns), F32),
            pltpu.VMEM((1, columns), F32),
            pltpu.VMEM((columns, depth), F32),
        ],
        compiler_params=pltpu.CompilerParams(vmem_limit_bytes=24 * 2**20),
        name="attend",
    )(first, count, bounds, q, new_keys, new_values, cache_keys, cache_values)
    out = out.reshape(windows, kv, span, padded, HD)[:, :, :, :group]
    return out.transpose(0, 2, 1, 3, 4).reshape(tokens, kv * group * HD)


def per_device(
    queries, new_keys, new_values, cache_keys, cache_values, tok_req, cache_req,
    out_weight, residual, norm_gain, gate_weight, up_weight, down_weight,
):
    attended = attend(queries, new_keys, new_values, cache_keys, cache_values, tok_req, cache_req)
    partial_out = jnp.dot(
        lax.all_gather(attended, "req", axis=0, tiled=True),
        out_weight,
        preferred_element_type=F32,
    )
    mixed = lax.psum_scatter(
        partial_out.astype(BF), "tp", scatter_dimension=0, tiled=True
    ).astype(F32)
    stream = (residual.astype(F32) + mixed).astype(BF)
    whole = lax.all_gather(stream, "req", axis=1, tiled=True)
    whole = lax.all_gather(whole, "tp", axis=0, tiled=True).astype(F32)
    mean_square = jnp.mean(whole * whole, axis=1, keepdims=True)
    normed = (whole * lax.rsqrt(mean_square + epsilon) * norm_gain[None, :]).astype(BF)
    gate = jnp.dot(normed, gate_weight, preferred_element_type=F32)
    up = jnp.dot(normed, up_weight, preferred_element_type=F32)
    hidden = (jax.nn.silu(gate) * up).astype(BF)
    product = jnp.dot(hidden, down_weight, preferred_element_type=F32)
    summed = lax.psum_scatter(product, "tp", scatter_dimension=0, tiled=True)
    summed = lax.psum_scatter(summed, "req", scatter_dimension=1, tiled=True)
    return (stream.astype(F32) + summed).astype(BF)


def solution(mesh):
    in_specs = (
        P("req", "tp"),
        P("req", "tp"),
        P("req", "tp"),
        P("req", "tp"),
        P("req", "tp"),
        P("req"),
        P("req"),
        P("tp", "req"),
        P("tp", "req"),
        P(),
        P(None, ("req", "tp")),
        P(None, ("req", "tp")),
        P(("req", "tp"), None),
    )
    out_specs = P("tp", "req")
    return jax.shard_map(
        per_device, mesh=mesh, in_specs=in_specs, out_specs=out_specs, check_vma=False
    )
```

time: 611 us -> 344 us (0.56)
  blocking collectives: 220 us -> 81.2 us
  matrix products: 96.1 us -> 27.1 us
  local copies, waits for them, and re-layouts: 74.9 us -> 15.2 us
  other arithmetic: 32.9 us -> 12.4 us
  waiting for transfers between devices: 172 us -> 187 us
  Pallas kernels: 0 us -> 7.7 us
    all_gather x1, blocking collectives: 198 us -> 46.8 us  [per_device(): lax.all_gather(attended, 'req', axis=0, tiled=True)]
    dot_general x43 -> x2, matrix products: 94.2 us -> 25.1 us  [the longest x1 16.5 us: per_device(): product = jnp.dot(hidden, down_weight, preferred_element_type=F32)]
    all_gather x0 -> x1, blocking collectives: none -> 34.4 us  [per_device(): whole = lax.all_gather(stream, 'req', axis=1, tiled=True)]
    all_gather x1, waiting for transfers between devices: 4.25 us -> 31.6 us  [per_device(): whole = lax.all_gather(whole, 'tp', axis=0, tiled=True).astype(F32)]
    gather x3 -> x0, local copies, waits for them, and re-layouts: 26.7 us -> none  [the longest x1 8.93 us: per_device(): gate_blocks[column_ids]]
    psum x1 -> x0, blocking collectives: 21.4 us -> none  [per_device(): squares = lax.psum(jnp.sum(wide * wide, axis=1), 'req')]
    scatter-add x2 -> x0, other arithmetic: 12.7 us -> none  [per_device(): zeros.reshape(total_tokens // sub_rows, sub_rows, hidden_here).at[token_ids]]
    reduce_scatter x2 -> x3, waiting for transfers between devices: 168 us -> 155 us  [the longest x1 69.9 us: per_device(): summed = lax.psum_scatter(summed, 'req', scatter_dimension=1, tiled=True)]
  transfers between devices with their start and end apart: 3 -> 4, of which waited for: 3 -> 4; matrix products, arithmetic and copies ran while one was open for 9% -> 0% of each run, Pallas kernels for 0% -> 0%
where the time goes in v1:
time: 344 us
  waiting for transfers between devices  187 us (54%)
  blocking collectives  81.2 us (24%)
  matrix products  27.1 us (8%)
  local copies, waits for them, and re-layouts  15.2 us (4%)
  between operations  13.2 us (4%)
  other arithmetic  12.4 us (4%)
  Pallas kernels  7.7 us (2%)
    reduce_scatter x1, waiting for transfers between devices, per_device(): summed = lax.psum_scatter(summed, 'req', scatter_dimension=1, tiled=True)  69.9 us
    reduce_scatter x1, waiting for transfers between devices, per_device(): summed = lax.psum_scatter(product, 'tp', scatter_dimension=0, tiled=True)  65.5 us
    all_gather x1, blocking collectives, per_device(): lax.all_gather(attended, 'req', axis=0, tiled=True)  46.8 us
    all_gather x1, blocking collectives, per_device(): whole = lax.all_gather(stream, 'req', axis=1, tiled=True)  34.4 us
    all_gather x1, waiting for transfers between devices, per_device(): whole = lax.all_gather(whole, 'tp', axis=0, tiled=True).astype(F32)  31.6 us
    reduce_scatter x1, waiting for transfers between devices, per_device(): lax.psum_scatter(partial_out.astype(BF), 'tp', scatter_dimension=0, tiled...  19.8 us
    dot_general x1, matrix products, per_device(): product = jnp.dot(hidden, down_weight, preferred_element_type=F32)  16.5 us
    unnamed x24, local copies, waits for them, and re-layouts  8.73 us
  transfers between devices with their start and end apart: 4, of which 4 were waited for; matrix products, arithmetic and copies ran while one was open for 0% of the time, Pallas kernels for 0%

profile of v1, /device:TPU:0, one launch (start us, length us, event | category | flops | bytes accessed | tf_op | source)
XLA Modules:
  0.0 344.0 jit_solution(16640120819809888141)
XLA Ops:
  6.5 1.0 convert_reduce_fusion.2
  7.5 0.9 broadcast_compare_fusion
  8.5 1.7 convert_reduce_fusion
  11.9 0.9 pad_bitcast_fusion
  12.9 0.9 mul.53
  13.7 1.1 mul.54
  15.6 1.1 reshape.80.bounds_ref
  16.7 1.4 reduce_max.9
  18.1 1.3 reduce_min.9
  20.2 3.6 %copy-done.2 = bf16[17920,256]{1,0:T(8,128)(2,1)S(1)} copy-done((bf16[17920,256]{1,0:T(8,128)(2,1)S(1)}, bf16[17920,256]{1,0:T(8,128)(2,1)}, u32[]{:S(2)}) %copy-start.2) | copy-done | bytes 9175064
  23.7 3.6 %copy-done.3 = bf16[17920,256]{1,0:T(8,128)(2,1)S(1)} copy-done((bf16[17920,256]{1,0:T(8,128)(2,1)S(1)}, bf16[17920,256]{1,0:T(8,128)(2,1)}, u32[]{:S(2)}) %copy-start.3) | copy-done | bytes 9175064
  28.8 7.7 %attend.1 = bf16[4,128,128]{2,1,0:T(8,128)(2,1)S(1)} custom-call(s32[4]{0:T(128)S(1)} %get-tuple-element.8.first_ref, s32[4]{0:T(128)S(1)} %get-tuple-element.7.count_ref, s32[4,8,128]{2,1,0:T(8,128)S(1)} %reshape.80.bounds_ref, bf16[4,128,256]{2,1,0:T(8,128)(2,1)S(1)} %broadcast_multiply_fusion.q_ref, bf16[32,256]{1,0:T(8,128)(2,1)S(1)} %copy-done.4, ...), custom_call_target="tpu_custom_call" | custom-call | tf_op jit(solution)/shard_map/attend/pallas_call | solution.py:140
  36.5 46.8 %all_gather.9 = bf16[256,1792]{1,0:T(8,128)(2,1)S(1)} all-gather(bf16[32,1792]{1,0:T(8,128)(2,1)S(1)} %bitcast.33), channel_id=1, replica_groups=mesh['req'=8,'tp'=4] {'req'}, dimensions={0}, use_global_device_ids=true | all-gather | bytes 1032192 | tf_op jit(solution)/shard_map/all_gather | solution.py:167
  83.3 1.9 convolution_convert_fusion
  85.3 19.8 %reduce-scatter.4.cloned.1.call-done = bf16[64,896]{1,0:T(8,128)(2,1)} async-done(((bf16[256,896]{1,0:T(8,128)(2,1)}), bf16[64,896]{1,0:T(8,128)(2,1)}) %reduce-scatter.4.cloned.1.call-update) | async-done | bytes 114704 | tf_op jit(solution)/shard_map/reduce_scatter | solution.py:171
  105.1 0.9 add_convert_fusion.1
  106.1 34.4 %all_gather.10 = bf16[64,7168]{1,0:T(8,128)(2,1)} all-gather(bf16[64,896]{1,0:T(8,128)(2,1)S(1)} %add_convert_fusion.1), channel_id=1, replica_groups=mesh['req'=8,'tp'=4] {'req'}, dimensions={1}, use_global_device_ids=true | all-gather | bytes 1032192 | tf_op jit(solution)/shard_map/all_gather | solution.py:175
  140.8 31.6 %all-gather.2.cloned.1.call-done = bf16[256,7168]{1,0:T(8,128)(2,1)} async-done(((bf16[64,7168]{1,0:T(8,128)(2,1)}), bf16[256,7168]{1,0:T(8,128)(2,1)}) %all-gather.2.cloned.1.call-update) | async-done | bytes 3670032 | tf_op jit(solution)/shard_map/all_gather | solution.py:176
  172.3 2.8 fusion
  175.2 8.7 %fusion.5 = f32[256,640]{1,0:T(8,128)} fusion(bf16[7168,640]{1,0:T(8,128)(2,1)} %param.23, bf16[256,7168]{1,0:T(8,128)(2,1)} %all-gather.2.cloned.1.call-done, f32[7168]{0:T(1024)S(1)} %copy-done.7, f32[256]{0:T(256)S(1)} %add_rsqrt_fusion), kind=kOutput, calls=%fused_computation.10 | convolution fusion | flops 2356150272 | bytes 13530112 | tf_op jit(solution)/shard_map/dot_general | solution.py:179
  183.9 16.5 %fusion.10 = f32[256,7168]{1,0:T(8,128)} fusion(bf16[640,7168]{1,0:T(8,128)(2,1)} %param.25, bf16[7168,640]{1,0:T(8,128)(2,1)} %param.24, bf16[256,7168]{1,0:T(8,128)(2,1)} %all-gather.2.cloned.1.call-done, f32[7168]{0:T(1024)S(1)} %copy-done.7, f32[256]{0:T(256)S(1)} %add_rsqrt_fusion, f32[256,640]{1,0:T(8,128)} %fusion.5), kind=kOutput, calls=%fused_computation.40 | convolution fusion | flops 4705943552 | bytes 30045184 | tf_op jit(solution)/shard_map/dot_general | solution.py:182
  200.4 65.5 %reduce-scatter.6.cloned.1.call-done = f32[64,7168]{1,0:T(8,128)} async-done(((f32[256,7168]{1,0:T(8,128)}), f32[64,7168]{1,0:T(8,128)}) %reduce-scatter.6.cloned.1.call-update) | async-done | bytes 1835024 | tf_op jit(solution)/shard_map/reduce_scatter | solution.py:183
  266.0 69.9 %reduce-scatter.8.cloned.1.call-done = f32[64,896]{1,0:T(8,128)} async-done(((f32[64,7168]{1,0:T(8,128)}), f32[64,896]{1,0:T(8,128)}) %reduce-scatter.8.cloned.1.call-update) | async-done | bytes 229392 | tf_op jit(solution)/shard_map/reduce_scatter | solution.py:184
  335.9 1.6 add_convert_fusion
  (45 shorter events, 5.2 us)
Async XLA Ops:
  6.5 76.8 %copy-start = (bf16[1792,896]{1,0:T(8,128)(2,1)S(1)}, bf16[1792,896]{1,0:T(8,128)(2,1)}, u32[]{:S(2)}) copy-start(bf16[1792,896]{1,0:T(8,128)(2,1)} %param.20) | copy-start | bytes 9633796
  6.5 98.6 %reduce-scatter.4.cloned.1.call-start = ((), (), s32[]{:S(2)}) async-start(), calls=%async_computation.3 | async-start | bytes 573440 | tf_op jit(solution)/shard_map/reduce_scatter | solution.py:171
  20.1 3.6 %copy-start.2 = (bf16[17920,256]{1,0:T(8,128)(2,1)S(1)}, bf16[17920,256]{1,0:T(8,128)(2,1)}, u32[]{:S(2)}) copy-start(bf16[17920,256]{1,0:T(8,128)(2,1)} %ck_ref.1) | copy-start | bytes 27525124
  23.7 3.6 %copy-start.3 = (bf16[17920,256]{1,0:T(8,128)(2,1)S(1)}, bf16[17920,256]{1,0:T(8,128)(2,1)}, u32[]{:S(2)}) copy-start(bf16[17920,256]{1,0:T(8,128)(2,1)} %cv_ref.1) | copy-start | bytes 27525124
  27.4 0.7 copy-start.4
  28.1 0.7 copy-start.5
  36.5 68.6 %copy-start.6 = (bf16[64,896]{1,0:T(8,128)(2,1)S(1)}, bf16[64,896]{1,0:T(8,128)(2,1)}, u32[]{:S(2)}) copy-start(bf16[64,896]{1,0:T(8,128)(2,1)} %param.21) | copy-start | bytes 344068
  36.5 138.7 %copy-start.7 = (f32[7168]{0:T(1024)S(1)}, f32[7168]{0:T(1024)}, u32[]{:S(2)}) copy-start(f32[7168]{0:T(1024)} %param.22) | copy-start | bytes 86020
  85.3 87.0 %all-gather.2.cloned.1.call-start = ((), (), s32[]{:S(2)}) async-start(), calls=%async_computation.4 | async-start | bytes 4587520 | tf_op jit(solution)/shard_map/all_gather | solution.py:176
  140.5 125.4 %reduce-scatter.6.cloned.1.call-start = ((), (), s32[]{:S(2)}) async-start(), calls=%async_computation.5 | async-start | bytes 9175040 | tf_op jit(solution)/shard_map/reduce_scatter | solution.py:183
  183.8 153.6 %copy-start.1 = (bf16[1792,896]{1,0:T(8,128)(2,1)S(1)}, bf16[1792,896]{1,0:T(8,128)(2,1)}, u32[]{:S(2)}) copy-start(bf16[1792,896]{1,0:T(8,128)(2,1)} %param.20) | copy-start | bytes 9633796
  200.4 135.5 %reduce-scatter.8.cloned.1.call-start = ((), (), s32[]{:S(2)}) async-start(), calls=%async_computation.6 | async-start | bytes 2064384 | tf_op jit(solution)/shard_map/reduce_scatter | solution.py:184
Sparse Core Ops, SparseCore 0:
  85.4 19.6 reduce-scatter.3
  140.6 31.6 all-gather.1
  200.5 65.4 reduce-scatter.5
  269.7 66.1 reduce-scatter.7

commit v2 on v1

--- a/solution.py
+++ b/solution.py
@@ -158,11 +158,263 @@
     return out.transpose(0, 2, 1, 3, 4).reshape(tokens, kv * group * HD)
 
 
+MESH = pl.DeviceIdType.MESH
+ZS = 4
+shrink = 2.0**-24
+
+
+def rest_kernel(
+    att_ref, ow_hbm, res_ref, gain_ref, gw_hbm, uw_hbm, dw_hbm, out_ref,
+    att, ow, gw, uw, dw, part, core_in, y_out, y_in, flow, gate_acc, up_acc, square_acc,
+    hidden, prod, prod_core, diag_y, diag_x, from_x, from_y, from_z,
+    local, send_sem, recv_sem,
+):
+    req, tp = lax.axis_index("req"), lax.axis_index("tp")
+    z, x, y, c = req // 2, lax.rem(req, 2), tp // 2, lax.rem(tp, 2)
+    columns = out_ref.shape[1]
+    rows = out_ref.shape[0]
+    half = rows // 2
+    reqs = flow.shape[0]
+    tokens = rows * flow.shape[1]
+    upper, lower = pl.ds(0, half), pl.ds(half, half)
+
+    loads = [
+        pltpu.make_async_copy(ow_hbm, ow, local.at[0]),
+        pltpu.make_async_copy(gw_hbm, gw, local.at[1]),
+        pltpu.make_async_copy(uw_hbm, uw, local.at[2]),
+    ]
+    for r in range(reqs):
+        part_cols = pl.ds(r * columns, columns)
+        loads.append(pltpu.make_async_copy(dw_hbm.at[:, part_cols], dw.at[r], local.at[3 + r]))
+    for load in loads:
+        load.start()
+
+    core_peer = (req, y * 2 + 1 - c)
+    y_peer = (req, (1 - y) * 2 + c)
+    x_peer = (z * 2 + 1 - x, tp)
+
+    def z_peer(k):
+        return (lax.rem(z + k, ZS) * 2 + x, tp)
+
+    barrier = pltpu.get_barrier_semaphore()
+    peers = [core_peer, y_peer, x_peer] + [z_peer(k) for k in range(1, ZS)]
+    for peer in peers:
+        pl.semaphore_signal(barrier, inc=1, device_id=peer, device_id_type=MESH)
+    pl.semaphore_wait(barrier, len(peers))
+
+    sent = []
+
+    def send(src, dst, peer):
+        i = len(sent)
+        copy = pltpu.make_async_remote_copy(
+            src_ref=src, dst_ref=dst, send_sem=send_sem.at[i], recv_sem=recv_sem.at[i],
+            device_id=peer, device_id_type=MESH,
+        )
+        copy.start()
+        sent.append(copy)
+        return copy
+
+    def behind(k):
+        return lax.rem(z - k + ZS, ZS)
+
+    along_z = [None] + [send(att_ref, att.at[req], z_peer(k)) for k in range(1, ZS)]
+    across = [send(att_ref, att.at[req], x_peer)]
+    att[req] = att_ref[...]
+    for k in range(1, ZS):
+        along_z[k].wait_recv()
+        block = att.at[behind(k) * 2 + x]
+        across.append(send(block, block, x_peer))
+    for copy in across:
+        copy.wait_recv()
+    loads[0].wait()
+    mixed = jnp.dot(
+        att[...].reshape(tokens, att.shape[2]), ow[...], preferred_element_type=F32
+    ).astype(BF).reshape(flow.shape[1], rows, columns)
+    for cc in range(2):
+        for yy in range(2):
+            part[cc, yy] = mixed[yy * 2 + cc]
+    copy = send(part.at[1 - c], core_in, core_peer)
+    copy.wait_recv()
+    y_out[...] = (part[c, 1 - y].astype(F32) + core_in[1 - y].astype(F32)).astype(BF)
+    copy = send(y_out, y_in, y_peer)
+    kept = part[c, y].astype(F32) + core_in[y].astype(F32)
+    copy.wait_recv()
+    stream = (res_ref[...].astype(F32) + (kept + y_in[...].astype(F32))).astype(BF)
+    flow[req, tp] = stream
+
+    def place(zz, xx, yy):
+        return flow.at[zz * 2 + xx, yy * 2 + c]
+
+    own = flow.at[req, tp]
+    along_z = [None] + [send(own, own, z_peer(k)) for k in range(1, ZS)]
+    to_x, to_y, turn_y, turn_x = {}, {}, {}, {}
+    to_core = {k: [] for k in range(ZS)}
+    gate_acc[...] = jnp.zeros_like(gate_acc)
+    up_acc[...] = jnp.zeros_like(up_acc)
+    square_acc[...] = jnp.zeros_like(square_acc)
+    for t in range(ZS + 3):
+        k = t
+        if k < ZS:
+            if k > 0:
+                along_z[k].wait_recv()
+            block = place(behind(k), x, y)
+            to_x[k] = send(block, block, x_peer)
+            to_y[k] = send(block, block, y_peer)
+            to_core[k].append(send(block, block, core_peer))
+        k = t - 1
+        if 0 <= k < ZS:
+            to_x[k].wait_recv()
+            block = place(behind(k), 1 - x, y)
+            turn_y[k] = send(block.at[upper], block.at[upper], y_peer)
+            to_core[k].append(send(block, block, core_peer))
+            to_y[k].wait_recv()
+            block = place(behind(k), x, 1 - y)
+            turn_x[k] = send(block.at[lower], block.at[lower], x_peer)
+            to_core[k].append(send(block, block, core_peer))
+        k = t - 2
+        if 0 <= k < ZS:
+            turn_y[k].wait_recv()
+            turn_x[k].wait_recv()
+            block = place(behind(k), 1 - x, 1 - y)
+            to_core[k].append(send(block, block, core_peer))
+        k = t - 3
+        if 0 <= k < ZS:
+            for copy in to_core[k]:
+                copy.wait_recv()
+            if k == 0:
+                loads[1].wait()
+                loads[2].wait()
+
+            def feed(xx, unused):
+                r = behind(k) * 2 + xx
+                wide = flow[r].astype(F32).reshape(tokens, columns)
+                square_acc[...] += jnp.sum(wide * wide, axis=1, keepdims=True)
+                gained = (wide * (gain_ref[r] * shrink)).astype(BF)
+                depth = pl.ds(pl.multiple_of(r * columns, columns), columns)
+                gate_acc[...] += jnp.dot(gained, gw[depth, :], preferred_element_type=F32)
+                up_acc[...] += jnp.dot(gained, uw[depth, :], preferred_element_type=F32)
+                return unused
+
+            lax.fori_loop(0, 2, feed, 0)
+
+    scale = lax.rsqrt(square_acc[...] / (columns * reqs) + epsilon) * (1.0 / shrink)
+    gate = gate_acc[...] * scale
+    hidden[...] = (gate / (1.0 + jnp.exp(-gate)) * (up_acc[...] * scale)).astype(BF)
+    for load in loads[3:]:
+        load.wait()
+
+    def ahead(k):
+        return lax.rem(z + k, ZS)
+
+    order = list(range(1, ZS)) + [0]
+    to_core, turn_y, turn_x, to_x, to_y, along_z = {}, {}, {}, {}, {}, []
+    for t in range(ZS + 3):
+        j = t
+        if j < ZS:
+            to_core[j] = []
+            for xx in range(2):
+                r = ahead(order[j]) * 2 + xx
+                term = jnp.dot(hidden[...], dw[r], preferred_element_type=F32)
+                term = term.astype(BF).reshape(flow.shape[1], rows, columns)
+                for cc in range(2):
+                    for yy in range(2):
+                        prod[r, cc, yy] = term[yy * 2 + cc]
+                to_core[j].append(send(prod.at[r, 1 - c], prod_core.at[r], core_peer))
+        j = t - 1
+        if 0 <= j < ZS:
+            for xx in range(2):
+                r = ahead(order[j]) * 2 + xx
+                to_core[j][xx].wait_recv()
+                prod[r, c] = (prod[r, c].astype(F32) + prod_core[r].astype(F32)).astype(BF)
+            block = prod.at[ahead(order[j]) * 2 + 1 - x, c, 1 - y]
+            turn_y[j] = send(block.at[upper], diag_y.at[j], y_peer)
+            turn_x[j] = send(block.at[lower], diag_x.at[j], x_peer)
+        j = t - 2
+        if 0 <= j < ZS:
+            turn_y[j].wait_recv()
+            block = prod.at[ahead(order[j]) * 2 + 1 - x, c, y]
+            block[upper] = (block[upper].astype(F32) + diag_y[j].astype(F32)).astype(BF)
+            to_x[j] = send(block, from_x.at[j], x_peer)
+            turn_x[j].wait_recv()
+            block = prod.at[ahead(order[j]) * 2 + x, c, 1 - y]
+            block[lower] = (block[lower].astype(F32) + diag_x[j].astype(F32)).astype(BF)
+            to_y[j] = send(block, from_y.at[j], y_peer)
+        j = t - 3
+        if 0 <= j < ZS:
+            to_x[j].wait_recv()
+            to_y[j].wait_recv()
+            block = prod.at[ahead(order[j]) * 2 + x, c, y]
+            total = block[...].astype(F32) + (from_x[j].astype(F32) + from_y[j].astype(F32))
+            if order[j] > 0:
+                block[...] = total.astype(BF)
+                along_z.append(send(block, from_z.at[j], z_peer(order[j])))
+    for j, copy in enumerate(along_z):
+        copy.wait_recv()
+        total = total + from_z[j].astype(F32)
+    out_ref[...] = (flow[req, tp].astype(F32) + total).astype(BF)
+    for copy in sent:
+        copy.wait_send()
+
+
+def rest(attended, out_weight, residual, norm_gain, gate_weight, up_weight, down_weight, reqs, tps):
+    rows, columns = residual.shape
+    tokens, depth = attended.shape
+    hidden_here = gate_weight.shape[1]
+    vmem = pl.BlockSpec(memory_space=pltpu.VMEM)
+    anywhere = pl.BlockSpec(memory_space=pl.ANY)
+    copies = 2 * ZS + 1 + (ZS - 1) + 8 * ZS + 6 * ZS + (ZS - 1)
+    half = rows // 2
+    return pl.pallas_call(
+        rest_kernel,
+        out_shape=jax.ShapeDtypeStruct((rows, columns), BF),
+        in_specs=[vmem, anywhere, vmem, vmem, anywhere, anywhere, anywhere],
+        out_specs=vmem,
+        scratch_shapes=[
+            pltpu.VMEM((reqs, tokens, depth), BF),
+            pltpu.VMEM(out_weight.shape, BF),
+            pltpu.VMEM(gate_weight.shape, BF),
+            pltpu.VMEM(up_weight.shape, BF),
+            pltpu.VMEM((reqs, hidden_here, columns), BF),
+            pltpu.VMEM((2, 2, rows, columns), BF),
+            pltpu.VMEM((2, rows, columns), BF),
+            pltpu.VMEM((rows, columns), BF),
+            pltpu.VMEM((rows, columns), BF),
+            pltpu.VMEM((reqs, tps, rows, columns), BF),
+            pltpu.VMEM((rows * tps, hidden_here), F32),
+            pltpu.VMEM((rows * tps, hidden_here), F32),
+            pltpu.VMEM((rows * tps, 1), F32),
+            pltpu.VMEM((rows * tps, hidden_here), BF),
+            pltpu.VMEM((reqs, 2, 2, rows, columns), BF),
+            pltpu.VMEM((reqs, 2, rows, columns), BF),
+            pltpu.VMEM((ZS, half, columns), BF),
+            pltpu.VMEM((ZS, half, columns), BF),
+            pltpu.VMEM((ZS, rows, columns), BF),
+            pltpu.VMEM((ZS, rows, columns), BF),
+            pltpu.VMEM((ZS - 1, rows, columns), BF),
+            pltpu.SemaphoreType.DMA((3 + reqs,)),
+            pltpu.SemaphoreType.DMA((copies,)),
+            pltpu.SemaphoreType.DMA((copies,)),
+        ],
+        compiler_params=pltpu.CompilerParams(
+            collective_id=0, has_side_effects=True, vmem_limit_bytes=60 * 2**20
+        ),
+        name="rest",
+    )(
+        attended, out_weight, residual, norm_gain.reshape(reqs, 1, columns),
+        gate_weight, up_weight, down_weight,
+    )
+
+
 def per_device(
     queries, new_keys, new_values, cache_keys, cache_values, tok_req, cache_req,
     out_weight, residual, norm_gain, gate_weight, up_weight, down_weight,
 ):
     attended = attend(queries, new_keys, new_values, cache_keys, cache_values, tok_req, cache_req)
+    reqs, tps = lax.axis_size("req"), lax.axis_size("tp")
+    if reqs == 2 * ZS and tps == 4 and residual.shape[0] % 32 == 0 and residual.shape[1] % 128 == 0:
+        return rest(
+            attended, out_weight, residual, norm_gain, gate_weight, up_weight, down_weight, reqs, tps
+        )
     partial_out = jnp.dot(
         lax.all_gather(attended, "req", axis=0, tiled=True),
         out_weight,

time: 344 us -> 116 us (0.34)
  waiting for transfers between devices: 187 us -> 0 us
  Pallas kernels: 7.7 us -> 97.4 us
  blocking collectives: 81.2 us -> 0 us
  matrix products: 27.1 us -> 0 us
  between operations: 13.2 us -> 0.11 us
  other arithmetic: 12.4 us -> 3.81 us
    reduce_scatter x3 -> x0, waiting for transfers between devices: 155 us -> none  [the longest x1 69.9 us: per_device(): summed = lax.psum_scatter(summed, 'req', scatter_dimension=1, tiled=True)]
    all_gather x2 -> x0, blocking collectives: 81.2 us -> none  [the longest x1 46.8 us: per_device(): lax.all_gather(attended, 'req', axis=0, tiled=True)]
    pallas_call x0 -> x1, Pallas kernels: none -> 78.8 us  [rest(): pl.pallas_call(rest_kernel, out_shape=jax.ShapeDtypeStruct((rows, columns...]
    all_gather x1 -> x0, waiting for transfers between devices: 31.6 us -> none  [per_device(): whole = lax.all_gather(whole, 'tp', axis=0, tiled=True).astype(F32)]
    dot_general x3 -> x0, matrix products: 27.1 us -> none  [the longest x1 16.5 us: per_device(): product = jnp.dot(hidden, down_weight, preferred_element_type=F32)]
    pallas_call x1, Pallas kernels: 7.7 us -> 18.7 us  [attend(): pl.pallas_call(attend_kernel, out_shape=jax.ShapeDtypeStruct((windows, co...]
    unnamed x24 -> x17, local copies, waits for them, and re-layouts: 8.73 us -> 10.9 us
  transfers between devices with their start and end apart: 4 -> 0, of which waited for: 4 -> 0; matrix products, arithmetic and copies ran while one was open for 0% -> 0% of each run, Pallas kernels for 0% -> 0%
where the time goes in v2:
time: 116 us; the launch traced here: 114 us
  Pallas kernels  97.4 us (84%)
  local copies, waits for them, and re-layouts  12.9 us (11%)
  other arithmetic  3.81 us (3%)
    pallas_call x1, Pallas kernels, rest(): pl.pallas_call(rest_kernel, out_shape=jax.ShapeDtypeStruct((rows, columns...  78.8 us
    pallas_call x1, Pallas kernels, attend(): pl.pallas_call(attend_kernel, out_shape=jax.ShapeDtypeStruct((windows, co...  18.7 us
    unnamed x17, local copies, waits for them, and re-layouts  10.9 us

profile of v2, /device:TPU:0, one launch (start us, length us, event | category | flops | bytes accessed | tf_op | source)
XLA Modules:
  0.0 114.3 jit_solution(8883849026698764621)
XLA Ops:
  0.0 0.9 broadcast_compare_fusion
  0.9 1.7 %convert_reduce_fusion = (s32[32]{0:T(128)S(1)}, s32[32]{0:T(128)S(1)}) fusion(s32[17920]{0:T(1024)} %param.19, s32[32]{0:T(128)} %param.18, pred[17920]{0:T(1024)(128)(4,1)S(1)} %broadcast_compare_fusion), kind=kLoop, calls=%fused_computation | loop fusion | flops 4587456 | bytes 89984 | tf_op jit(solution)/shard_map/reduce_sum | solution.py:120
  2.6 0.1 stack.8
  2.7 0.1 stack.18
  2.8 0.9 convert_reduce_fusion.2
  3.7 0.1 stack.19
  3.8 0.1 broadcast_in_dim.5
  3.9 0.1 reshape.74.bounds_ref
  4.1 0.1 reshape.73
  4.2 0.1 reduce_max.9
  4.3 0.1 reshape.72
  4.4 0.1 reduce_min.9
  4.5 0.9 pad_bitcast_fusion
  5.5 0.1 mul.27
  5.6 0.2 mul.28
  5.8 0.1 mul.29
  6.0 3.6 %copy-done = bf16[17920,256]{1,0:T(8,128)(2,1)S(1)} copy-done((bf16[17920,256]{1,0:T(8,128)(2,1)S(1)}, bf16[17920,256]{1,0:T(8,128)(2,1)}, u32[]{:S(2)}) %copy-start) | copy-done | bytes 9175064
  9.6 3.6 %copy-done.1 = bf16[17920,256]{1,0:T(8,128)(2,1)S(1)} copy-done((bf16[17920,256]{1,0:T(8,128)(2,1)S(1)}, bf16[17920,256]{1,0:T(8,128)(2,1)}, u32[]{:S(2)}) %copy-start.1) | copy-done | bytes 9175064
  13.2 0.7 copy-done.2
  13.9 0.7 copy-done.3
  14.6 18.7 %attend.1 = bf16[4,128,128]{2,1,0:T(8,128)(2,1)S(1)} custom-call(s32[4]{0:T(128)S(1)} %get-tuple-element.8.first_ref, s32[4]{0:T(128)S(1)} %get-tuple-element.7.count_ref, s32[4,8,128]{2,1,0:T(8,128)S(1)} %reshape.74.bounds_ref, bf16[4,128,256]{2,1,0:T(8,128)(2,1)S(1)} %broadcast_multiply_fusion.q_ref, bf16[32,256]{1,0:T(8,128)(2,1)S(1)} %copy-done.2, ...), custom_call_target="tpu_custom_call" | custom-call | tf_op jit(solution)/shard_map/attend/pallas_call | solution.py:140
  33.3 0.7 copy.24
  34.0 78.8 %rest.1 = bf16[64,896]{1,0:T(8,128)(2,1)} custom-call(bf16[32,1792]{1,0:T(8,128)(2,1)} %bitcast.24, bf16[1792,896]{1,0:T(8,128)(2,1)} %ow_hbm.1, bf16[64,896]{1,0:T(8,128)(2,1)} %res_ref.1, f32[8,1,896]{2,1,0:T(1,128)} %bitcast.28, bf16[7168,640]{1,0:T(8,128)(2,1)} %gw_hbm.1, bf16[7168,640]{1,0:T(8,128)(2,1)} %uw_hbm.1, bf16[640,7168]{1,0:T(8,128)(2,1)} %dw_hbm.1), custom_call_target="tpu_custom_call" | custom-call | tf_op jit(solution)/shard_map/rest/pallas_call | solution.py:367
  112.7 1.6 %copy.38 = bf16[64,896]{1,0:T(8,128)(2,1)} copy(bf16[64,896]{1,0:T(8,128)(2,1)} %rest.1) | data formatting | bytes 229376
  (18 shorter events, 0.2 us)
Async XLA Ops:
  6.0 3.6 %copy-start = (bf16[17920,256]{1,0:T(8,128)(2,1)S(1)}, bf16[17920,256]{1,0:T(8,128)(2,1)}, u32[]{:S(2)}) copy-start(bf16[17920,256]{1,0:T(8,128)(2,1)} %ck_ref.1) | copy-start | bytes 27525124
  9.6 3.6 %copy-start.1 = (bf16[17920,256]{1,0:T(8,128)(2,1)S(1)}, bf16[17920,256]{1,0:T(8,128)(2,1)}, u32[]{:S(2)}) copy-start(bf16[17920,256]{1,0:T(8,128)(2,1)} %cv_ref.1) | copy-start | bytes 27525124
  13.2 0.7 copy-start.2
  13.9 0.7 copy-start.3

commit v3 on v2

--- a/solution.py
+++ b/solution.py
@@ -11,7 +11,7 @@
 HD = 128
 epsilon = 1e-05
 masked_value = -1e30
-key_block = 512
+key_block = 1024
 score_factor = math.log2(math.e) / math.sqrt(HD)
 BF = jnp.bfloat16
 F32 = jnp.float32
@@ -52,26 +52,23 @@
         fetch(w0, b0, i)
         w0, b0 = advance(w0, b0)
 
-    def col(row):
-        return jnp.transpose(jnp.broadcast_to(row, (8, row.shape[1])))[:, :1]
-
     def scores_of(keys, w, low, high):
         s = lax.dot_general(
-            keys, q_ref[w], (((1,), (1,)), ((), ())), preferred_element_type=F32
+            q_ref[w], keys, (((1,), (1,)), ((), ())), preferred_element_type=F32
         )
-        pos = lax.broadcasted_iota(jnp.int32, s.shape, 0)
+        pos = lax.broadcasted_iota(jnp.int32, s.shape, 1)
         return jnp.where((pos >= low) & (pos < high), s * score_factor, masked_value)
 
     def weigh(p, values):
-        return lax.dot_general(p, values, (((0,), (0,)), ((), ())), preferred_element_type=F32)
+        return jnp.dot(p, values, preferred_element_type=F32)
 
     def window(w, carry):
-        low, high = bounds_ref[w, 0:1, :], bounds_ref[w, 1:2, :]
-        s = scores_of(nk_ref[...], w, bounds_ref[w, 2:3, :], bounds_ref[w, 3:4, :])
-        m = jnp.max(s, axis=0, keepdims=True)
+        low, high = bounds_ref[w, :, 0:1], bounds_ref[w, :, 1:2]
+        s = scores_of(nk_ref[...], w, bounds_ref[w, :, 2:3], bounds_ref[w, :, 3:4])
+        m = jnp.max(s, axis=1, keepdims=True)
         p = jnp.exp2(s - m).astype(BF)
         m_ref[...] = m
-        l_ref[...] = jnp.sum(p.astype(F32), axis=0, keepdims=True)
+        l_ref[...] = jnp.sum(p.astype(F32), axis=1, keepdims=True)
         acc_ref[...] = weigh(p, nv_ref[...])
 
         def block(b, inner):
@@ -84,16 +81,16 @@
             start = jnp.minimum(nominal, pool - width)
             s = scores_of(kbuf[slot], w, jnp.maximum(low, nominal) - start, high - start)
             m_old = m_ref[...]
-            m_new = jnp.maximum(m_old, jnp.max(s, axis=0, keepdims=True))
+            m_new = jnp.maximum(m_old, jnp.max(s, axis=1, keepdims=True))
             alpha = jnp.exp2(m_old - m_new)
             p = jnp.exp2(s - m_new).astype(BF)
             m_ref[...] = m_new
-            l_ref[...] = l_ref[...] * alpha + jnp.sum(p.astype(F32), axis=0, keepdims=True)
-            acc_ref[...] = acc_ref[...] * col(alpha) + weigh(p, vbuf[slot])
+            l_ref[...] = l_ref[...] * alpha + jnp.sum(p.astype(F32), axis=1, keepdims=True)
+            acc_ref[...] = acc_ref[...] * alpha + weigh(p, vbuf[slot])
             return (item + 1, *advance(wn, bn))
 
         carry = lax.fori_loop(0, count_ref[w], block, carry)
-        scaled = acc_ref[...] / col(l_ref[...])
+        scaled = acc_ref[...] / l_ref[...]
         rows = scaled.shape[0] // kv
         for h in range(kv):
             part = slice(h * rows, (h + 1) * rows)
@@ -123,9 +120,8 @@
     first = jnp.min(low.reshape(windows, span), axis=1) // 16 * 16
     last = jnp.max(high.reshape(windows, span), axis=1)
     count = jnp.maximum((last - first + width - 1) // width, 1)
-    bounds = jnp.stack([low, high, new_low, new_high] * 2)
-    bounds = bounds.reshape(8, windows, 1, span, 1).transpose(1, 0, 2, 3, 4)
-    bounds = jnp.broadcast_to(bounds, (windows, 8, kv, span, padded)).reshape(windows, 8, columns)
+    bounds = jnp.stack([low, high, new_low, new_high], axis=1).reshape(windows, 1, span, 1, 4)
+    bounds = jnp.broadcast_to(bounds, (windows, kv, span, padded, 4)).reshape(windows, columns, 4)
 
     q = queries.reshape(windows, span, kv, group, HD)
     q = jnp.pad(q, ((0, 0), (0, 0), (0, 0), (0, padded - group), (0, 0)))
@@ -147,11 +143,11 @@
             pltpu.VMEM((slots, width, depth), BF),
             pltpu.SemaphoreType.DMA((slots,)),
             pltpu.SemaphoreType.DMA((slots,)),
-            pltpu.VMEM((1, columns), F32),
-            pltpu.VMEM((1, columns), F32),
+            pltpu.VMEM((columns, 1), F32),
+            pltpu.VMEM((columns, 1), F32),
             pltpu.VMEM((columns, depth), F32),
         ],
-        compiler_params=pltpu.CompilerParams(vmem_limit_bytes=24 * 2**20),
+        compiler_params=pltpu.CompilerParams(vmem_limit_bytes=60 * 2**20),
         name="attend",
     )(first, count, bounds, q, new_keys, new_values, cache_keys, cache_values)
     out = out.reshape(windows, kv, span, padded, HD)[:, :, :, :group]
@@ -308,46 +304,81 @@
 
     order = list(range(1, ZS)) + [0]
     to_core, turn_y, turn_x, to_x, to_y, along_z = {}, {}, {}, {}, {}, []
-    for t in range(ZS + 3):
-        j = t
-        if j < ZS:
-            to_core[j] = []
-            for xx in range(2):
-                r = ahead(order[j]) * 2 + xx
-                term = jnp.dot(hidden[...], dw[r], preferred_element_type=F32)
-                term = term.astype(BF).reshape(flow.shape[1], rows, columns)
-                for cc in range(2):
-                    for yy in range(2):
-                        prod[r, cc, yy] = term[yy * 2 + cc]
-                to_core[j].append(send(prod.at[r, 1 - c], prod_core.at[r], core_peer))
-        j = t - 1
-        if 0 <= j < ZS:
-            for xx in range(2):
-                r = ahead(order[j]) * 2 + xx
-                to_core[j][xx].wait_recv()
-                prod[r, c] = (prod[r, c].astype(F32) + prod_core[r].astype(F32)).astype(BF)
-            block = prod.at[ahead(order[j]) * 2 + 1 - x, c, 1 - y]
-            turn_y[j] = send(block.at[upper], diag_y.at[j], y_peer)
-            turn_x[j] = send(block.at[lower], diag_x.at[j], x_peer)
-        j = t - 2
-        if 0 <= j < ZS:
-            turn_y[j].wait_recv()
-            block = prod.at[ahead(order[j]) * 2 + 1 - x, c, y]
-            block[upper] = (block[upper].astype(F32) + diag_y[j].astype(F32)).astype(BF)
-            to_x[j] = send(block, from_x.at[j], x_peer)
-            turn_x[j].wait_recv()
-            block = prod.at[ahead(order[j]) * 2 + x, c, 1 - y]
-            block[lower] = (block[lower].astype(F32) + diag_x[j].astype(F32)).astype(BF)
-            to_y[j] = send(block, from_y.at[j], y_peer)
-        j = t - 3
-        if 0 <= j < ZS:
-            to_x[j].wait_recv()
-            to_y[j].wait_recv()
-            block = prod.at[ahead(order[j]) * 2 + x, c, y]
-            total = block[...].astype(F32) + (from_x[j].astype(F32) + from_y[j].astype(F32))
-            if order[j] > 0:
-                block[...] = total.astype(BF)
-                along_z.append(send(block, from_z.at[j], z_peer(order[j])))
+
+    def multiply(j, xx):
+        r = ahead(order[j]) * 2 + xx
+        term = jnp.dot(hidden[...], dw[r], preferred_element_type=F32)
+        term = term.astype(BF).reshape(flow.shape[1], rows, columns)
+        for cc in range(2):
+            for yy in range(2):
+                prod[r, cc, yy] = term[yy * 2 + cc]
+        return send(prod.at[r, 1 - c], prod_core.at[r], core_peer)
+
+    def join_core(copy, r):
+        copy.wait_recv()
+        prod[r, c] = (prod[r, c].astype(F32) + prod_core[r].astype(F32)).astype(BF)
+
+    def far(j):
+        to_core[j, 0] = multiply(j, 1 - x)
+
+    def near(j):
+        to_core[j, 1] = multiply(j, x)
+
+    def turn(j):
+        r = ahead(order[j]) * 2 + 1 - x
+        join_core(to_core[j, 0], r)
+        block = prod.at[r, c, 1 - y]
+        turn_y[j] = send(block.at[upper], diag_y.at[j], y_peer)
+        turn_x[j] = send(block.at[lower], diag_x.at[j], x_peer)
+
+    def over_x(j):
+        turn_y[j].wait_recv()
+        block = prod.at[ahead(order[j]) * 2 + 1 - x, c, y]
+        block[upper] = (block[upper].astype(F32) + diag_y[j].astype(F32)).astype(BF)
+        to_x[j] = send(block, from_x.at[j], x_peer)
+
+    def over_y(j):
+        r = ahead(order[j]) * 2 + x
+        join_core(to_core[j, 1], r)
+        turn_x[j].wait_recv()
+        block = prod.at[r, c, 1 - y]
+        block[lower] = (block[lower].astype(F32) + diag_x[j].astype(F32)).astype(BF)
+        to_y[j] = send(block, from_y.at[j], y_peer)
+
+    def finish(j):
+        to_x[j].wait_recv()
+        to_y[j].wait_recv()
+        block = prod.at[ahead(order[j]) * 2 + x, c, y]
+        total = block[...].astype(F32) + (from_x[j].astype(F32) + from_y[j].astype(F32))
+        if order[j] > 0:
+            block[...] = total.astype(BF)
+            along_z.append(send(block, from_z.at[j], z_peer(order[j])))
+        return total
+
+    far(0)
+    far(1)
+    turn(0)
+    near(0)
+    turn(1)
+    far(2)
+    over_x(0)
+    over_y(0)
+    turn(2)
+    near(1)
+    over_x(1)
+    over_y(1)
+    far(3)
+    turn(3)
+    near(2)
+    finish(0)
+    over_x(2)
+    over_y(2)
+    near(3)
+    finish(1)
+    over_x(3)
+    over_y(3)
+    finish(2)
+    total = finish(3)
     for j, copy in enumerate(along_z):
         copy.wait_recv()
         total = total + from_z[j].astype(F32)

time: 116 us -> 107 us (0.922); the launches traced: 114 us -> 107 us
  local copies, waits for them, and re-layouts: 12.9 us -> 5.7 us
  Pallas kernels: 97.4 us -> 96.2 us
  other arithmetic: 3.81 us -> 5.01 us
    unnamed x17 -> x3, local copies, waits for them, and re-layouts: 10.9 us -> 3.13 us
    pallas_call x1, Pallas kernels: 78.8 us -> 77.4 us  [rest(): pl.pallas_call(rest_kernel, out_shape=jax.ShapeDtypeStruct((rows, columns...]
where the time goes in v3:
time: 107 us
  Pallas kernels  96.2 us (90%)
  local copies, waits for them, and re-layouts  5.7 us (5%)
  other arithmetic  5.01 us (5%)
    pallas_call x1, Pallas kernels, rest(): pl.pallas_call(rest_kernel, out_shape=jax.ShapeDtypeStruct((rows, columns...  77.4 us
    pallas_call x1, Pallas kernels, attend(): pl.pallas_call(attend_kernel, out_shape=jax.ShapeDtypeStruct((windows, co...  18.8 us
    unnamed x3, local copies, waits for them, and re-layouts  3.13 us

profile of v3, /device:TPU:0, one launch (start us, length us, event | category | flops | bytes accessed | tf_op | source)
XLA Modules:
  0.0 107.0 jit_solution(3699994219432496719)
XLA Ops:
  0.0 0.9 convert_reduce_fusion.2
  0.9 0.1 stack.15
  1.0 0.9 broadcast_compare_fusion
  1.9 1.7 %convert_reduce_fusion = (s32[32]{0:T(128)S(1)}, s32[32]{0:T(128)S(1)}) fusion(s32[17920]{0:T(1024)} %param.19, s32[32]{0:T(128)} %param.18, pred[17920]{0:T(1024)(128)(4,1)S(1)} %broadcast_compare_fusion), kind=kLoop, calls=%fused_computation | loop fusion | flops 4587456 | bytes 89984 | tf_op jit(solution)/shard_map/reduce_sum | solution.py:117
  3.6 0.1 stack.14
  3.7 0.1 reshape.65
  3.8 0.1 reduce_max.9
  3.9 0.1 stack.13
  4.0 0.1 reshape.64
  4.1 0.1 reduce_min.9
  4.2 0.5 fusion
  4.7 0.1 copy.25
  4.8 0.1 mul.29
  4.9 0.9 pad_bitcast_fusion
  5.9 0.1 mul.27
  6.0 0.2 mul.28
  6.2 0.7 broadcast_multiply_fusion.q_ref
  6.9 0.7 broadcast_in_dim.5
  7.6 18.8 %attend.1 = bf16[4,128,128]{2,1,0:T(8,128)(2,1)} custom-call(s32[4]{0:T(128)} %get-tuple-element.8.first_ref, s32[4]{0:T(128)} %get-tuple-element.7.count_ref, s32[4,128,4]{2,1,0:T(8,128)} %bitcast.20, bf16[4,128,256]{2,1,0:T(8,128)(2,1)} %broadcast_multiply_fusion.q_ref, bf16[32,256]{1,0:T(8,128)(2,1)} %nk_ref.1, bf16[32,256]{1,0:T(8,128)(2,1)} %nv_ref.1, ...), custom_call_target="tpu_custom_call" | custom-call | tf_op jit(solution)/shard_map/attend/pallas_call | solution.py:136
  26.5 1.6 %copy.30 = bf16[4,2,8,7,128]{4,2,3,1,0:T(8,128)(2,1)} copy(bf16[4,2,8,7,128]{4,3,2,1,0:T(8,128)(2,1)} %bitcast.21) | data formatting | bytes 229376
  28.0 77.4 %rest.1 = bf16[64,896]{1,0:T(8,128)(2,1)} custom-call(bf16[32,1792]{1,0:T(8,128)(2,1)} %bitcast.23, bf16[1792,896]{1,0:T(8,128)(2,1)} %ow_hbm.1, bf16[64,896]{1,0:T(8,128)(2,1)} %res_ref.1, f32[8,1,896]{2,1,0:T(1,128)} %bitcast.27, bf16[7168,640]{1,0:T(8,128)(2,1)} %gw_hbm.1, bf16[7168,640]{1,0:T(8,128)(2,1)} %uw_hbm.1, bf16[640,7168]{1,0:T(8,128)(2,1)} %dw_hbm.1), custom_call_target="tpu_custom_call" | custom-call | tf_op jit(solution)/shard_map/rest/pallas_call | solution.py:398
  105.4 1.6 %copy.37 = bf16[64,896]{1,0:T(8,128)(2,1)} copy(bf16[64,896]{1,0:T(8,128)(2,1)} %rest.1) | data formatting | bytes 229376
  (5 shorter events, 0.1 us)

commit v4 on v3

--- a/solution.py
+++ b/solution.py
@@ -19,10 +19,13 @@
 
 def attend_kernel(
     first_ref, count_ref, bounds_ref, q_ref, nk_ref, nv_ref, ck_ref, cv_ref, out_ref,
-    kbuf, vbuf, ksem, vsem, m_ref, l_ref, acc_ref,
+    kbuf, vbuf, ksem, vsem, m_ref, l_ref, acc_ref, wide_q, spread, placed, wide_out,
 ):
-    windows = q_ref.shape[0]
-    kv = q_ref.shape[2] // HD
+    windows = bounds_ref.shape[0]
+    kv = acc_ref.shape[1] // HD
+    span = q_ref.shape[0] // windows
+    padded = acc_ref.shape[0] // (kv * span)
+    group = q_ref.shape[1] // (kv * HD)
     pool = ck_ref.shape[0]
     width = kbuf.shape[1]
     slots = kbuf.shape[0]
@@ -52,9 +55,20 @@
         fetch(w0, b0, i)
         w0, b0 = advance(w0, b0)
 
-    def scores_of(keys, w, low, high):
+    wide_q[...] = q_ref[...].astype(F32)
+    spread[...] = jnp.zeros_like(spread)
+    placed[...] = jnp.zeros_like(placed)
+    per_head = span * padded
+
+    def head_rows(g):
+        return pl.ds(g, span, stride=padded)
+
+    def own(h):
+        return slice(h * per_head, (h + 1) * per_head), slice(h * HD, (h + 1) * HD)
+
+    def scores_of(keys, q, low, high):
         s = lax.dot_general(
-            q_ref[w], keys, (((1,), (1,)), ((), ())), preferred_element_type=F32
+            q, keys, (((1,), (1,)), ((), ())), preferred_element_type=F32
         )
         pos = lax.broadcasted_iota(jnp.int32, s.shape, 1)
         return jnp.where((pos >= low) & (pos < high), s * score_factor, masked_value)
@@ -64,7 +78,13 @@
 
     def window(w, carry):
         low, high = bounds_ref[w, :, 0:1], bounds_ref[w, :, 1:2]
-        s = scores_of(nk_ref[...], w, bounds_ref[w, :, 2:3], bounds_ref[w, :, 3:4])
+        tokens = pl.ds(pl.multiple_of(w * span, span), span)
+        for h in range(kv):
+            for g in range(group):
+                at = (h * group + g) * HD
+                spread[h, head_rows(g), :] = wide_q[tokens, at : at + HD]
+            placed[own(h)] = spread[h].astype(BF)
+        s = scores_of(nk_ref[...], placed[...], bounds_ref[w, :, 2:3], bounds_ref[w, :, 3:4])
         m = jnp.max(s, axis=1, keepdims=True)
         p = jnp.exp2(s - m).astype(BF)
         m_ref[...] = m
@@ -79,7 +99,7 @@
                 c.wait()
             nominal = first_ref[w] + b * width
             start = jnp.minimum(nominal, pool - width)
-            s = scores_of(kbuf[slot], w, jnp.maximum(low, nominal) - start, high - start)
+            s = scores_of(kbuf[slot], placed[...], jnp.maximum(low, nominal) - start, high - start)
             m_old = m_ref[...]
             m_new = jnp.maximum(m_old, jnp.max(s, axis=1, keepdims=True))
             alpha = jnp.exp2(m_old - m_new)
@@ -91,13 +111,15 @@
 
         carry = lax.fori_loop(0, count_ref[w], block, carry)
         scaled = acc_ref[...] / l_ref[...]
-        rows = scaled.shape[0] // kv
         for h in range(kv):
-            part = slice(h * rows, (h + 1) * rows)
-            out_ref[w, part, :] = scaled[part, h * HD : (h + 1) * HD].astype(BF)
+            spread[h] = scaled[own(h)]
+            for g in range(group):
+                at = (h * group + g) * HD
+                wide_out[tokens, at : at + HD] = spread[h, head_rows(g), :]
         return carry
 
     lax.fori_loop(0, windows, window, (jnp.int32(0), w0, b0))
+    out_ref[...] = wide_out[...].astype(BF)
 
 
 def attend(queries, new_keys, new_values, cache_keys, cache_values, tok_req, cache_req):
@@ -112,9 +134,9 @@
     pool = cache_keys.shape[0]
     width = min(key_block, pool)
 
-    owned = cache_req[None, :] >= 0
-    low = jnp.sum((owned & (cache_req[None, :] < tok_req[:, None])).astype(jnp.int32), axis=1)
-    high = jnp.sum((owned & (cache_req[None, :] <= tok_req[:, None])).astype(jnp.int32), axis=1)
+    owner = jnp.where(cache_req < 0, 2**30, cache_req)[None, :]
+    low = jnp.sum((owner < tok_req[:, None]).astype(jnp.int32), axis=1)
+    high = jnp.sum((owner <= tok_req[:, None]).astype(jnp.int32), axis=1)
     new_low = jnp.sum((tok_req[None, :] < tok_req[:, None]).astype(jnp.int32), axis=1)
     new_high = jnp.arange(1, tokens + 1, dtype=jnp.int32)
     first = jnp.min(low.reshape(windows, span), axis=1) // 16 * 16
@@ -123,19 +145,13 @@
     bounds = jnp.stack([low, high, new_low, new_high], axis=1).reshape(windows, 1, span, 1, 4)
     bounds = jnp.broadcast_to(bounds, (windows, kv, span, padded, 4)).reshape(windows, columns, 4)
 
-    q = queries.reshape(windows, span, kv, group, HD)
-    q = jnp.pad(q, ((0, 0), (0, 0), (0, 0), (0, padded - group), (0, 0)))
-    q = q.transpose(0, 2, 1, 3, 4).reshape(windows, kv, span * padded, 1, HD)
-    q = q * jnp.eye(kv, dtype=BF)[None, :, None, :, None]
-    q = q.reshape(windows, columns, depth)
-
     vmem = pl.BlockSpec(memory_space=pltpu.VMEM)
     smem = pl.BlockSpec(memory_space=pltpu.SMEM)
     anywhere = pl.BlockSpec(memory_space=pl.ANY)
     slots = 4
-    out = pl.pallas_call(
+    return pl.pallas_call(
         attend_kernel,
-        out_shape=jax.ShapeDtypeStruct((windows, columns, HD), BF),
+        out_shape=jax.ShapeDtypeStruct(queries.shape, BF),
         in_specs=[smem, smem, vmem, vmem, vmem, vmem, anywhere, anywhere],
         out_specs=vmem,
         scratch_shapes=[
@@ -146,12 +162,14 @@
             pltpu.VMEM((columns, 1), F32),
             pltpu.VMEM((columns, 1), F32),
             pltpu.VMEM((columns, depth), F32),
+            pltpu.VMEM(queries.shape, F32),
+            pltpu.VMEM((kv, span * padded, HD), F32),
+            pltpu.VMEM((columns, depth), BF),
+            pltpu.VMEM(queries.shape, F32),
         ],
         compiler_params=pltpu.CompilerParams(vmem_limit_bytes=60 * 2**20),
         name="attend",
-    )(first, count, bounds, q, new_keys, new_values, cache_keys, cache_values)
-    out = out.reshape(windows, kv, span, padded, HD)[:, :, :, :group]
-    return out.transpose(0, 2, 1, 3, 4).reshape(tokens, kv * group * HD)
+    )(first, count, bounds, queries, new_keys, new_values, cache_keys, cache_values)
 
 
 MESH = pl.DeviceIdType.MESH

time: 107 us -> 102 us (0.953)
  local copies, waits for them, and re-layouts: 5.7 us -> 2.78 us
  other arithmetic: 5.01 us -> 3.93 us
    pallas_call x1, Pallas kernels: 18.8 us -> 16.4 us  [attend(): pl.pallas_call(attend_kernel, out_shape=jax.ShapeDtypeStruct(queries.shap...]
    unnamed x3 -> x1, local copies, waits for them, and re-layouts: 3.13 us -> 1.55 us
    pallas_call x1, Pallas kernels: 77.4 us -> 78.9 us  [rest(): pl.pallas_call(rest_kernel, out_shape=jax.ShapeDtypeStruct((rows, columns...]
where the time goes in v4:
time: 102 us
  Pallas kernels  95.3 us (93%)
  other arithmetic  3.93 us (4%)
  local copies, waits for them, and re-layouts  2.78 us (3%)
    pallas_call x1, Pallas kernels, rest(): pl.pallas_call(rest_kernel, out_shape=jax.ShapeDtypeStruct((rows, columns...  78.9 us
    pallas_call x1, Pallas kernels, attend(): pl.pallas_call(attend_kernel, out_shape=jax.ShapeDtypeStruct(queries.shap...  16.4 us

profile of v4, /device:TPU:0, one launch (start us, length us, event | category | flops | bytes accessed | tf_op | source)
XLA Modules:
  0.0 102.1 jit_solution(16363262835973083264)
XLA Ops:
  0.0 0.9 convert_reduce_fusion.2
  0.9 0.1 stack.15
  1.0 0.9 compare_select_fusion
  1.9 1.3 %convert_reduce_fusion = (s32[32]{0:T(128)S(1)}, s32[32]{0:T(128)S(1)}) fusion(s32[17920]{0:T(1024)S(1)} %compare_select_fusion, s32[32]{0:T(128)} %param.18), kind=kLoop, calls=%fused_computation | loop fusion | flops 3440576 | bytes 72064 | tf_op jit(solution)/shard_map/reduce_sum | solution.py:139
  3.2 0.1 stack.14
  3.3 0.1 reshape.41
  3.3 0.1 reduce_max.9
  3.5 0.1 stack.13
  3.6 0.1 reshape.40
  3.6 0.1 reduce_min.9
  3.8 0.6 fusion
  4.4 0.1 copy.17
  4.5 0.7 broadcast_in_dim.18
  5.2 16.4 %attend.1.att_ref = bf16[32,1792]{1,0:T(8,128)(2,1)} custom-call(s32[4]{0:T(128)} %get-tuple-element.8.first_ref, s32[4]{0:T(128)} %get-tuple-element.7.count_ref, s32[4,128,4]{2,1,0:T(8,128)} %bitcast.4, bf16[32,1792]{1,0:T(8,128)(2,1)} %q_ref.1, bf16[32,256]{1,0:T(8,128)(2,1)} %nk_ref.1, bf16[32,256]{1,0:T(8,128)(2,1)} %nv_ref.1, ...), custom_call_target="tpu_custom_call" | custom-call | tf_op jit(solution)/shard_map/attend/pallas_call | solution.py:152
  21.5 78.9 %rest.1 = bf16[64,896]{1,0:T(8,128)(2,1)} custom-call(bf16[32,1792]{1,0:T(8,128)(2,1)} %attend.1.att_ref, bf16[1792,896]{1,0:T(8,128)(2,1)} %ow_hbm.1, bf16[64,896]{1,0:T(8,128)(2,1)} %res_ref.1, f32[8,1,896]{2,1,0:T(1,128)} %bitcast.5, bf16[7168,640]{1,0:T(8,128)(2,1)} %gw_hbm.1, bf16[7168,640]{1,0:T(8,128)(2,1)} %uw_hbm.1, bf16[640,7168]{1,0:T(8,128)(2,1)} %dw_hbm.1), custom_call_target="tpu_custom_call" | custom-call | tf_op jit(solution)/shard_map/rest/pallas_call | solution.py:416
  100.5 1.6 %copy.21 = bf16[64,896]{1,0:T(8,128)(2,1)} copy(bf16[64,896]{1,0:T(8,128)(2,1)} %rest.1) | data formatting | bytes 229376
  (2 shorter events, 0.0 us)
